TPU v7x, 32 devices: a whole 2x2x4 slice. The times are simulated.
32 devices in a mesh: gx: 2 (over x), gy: 4 (over z), gz: 4 (over y, core).
Axes of the slice: x: 2, y: 2, z: 4, core: 2. Of those that a mesh axis runs over, the one named last changes fastest.
Arguments:
- initial_block: float32 [64, 32, 32, 256], P(None, 'gz', 'gy', 'gx'), may hold values from -6 to 6
- phase_map: int32 [32, 32, 256], P('gz', 'gy', 'gx'), may hold values from 0 to 3
- phase_density: float32 [4], replicated, may hold values from 0.5 to 4
- phase_modulus: float32 [4], replicated, may hold values from 0.5 to 4
- bloch_sign: int32 [32, 256], P('gy', 'gx'), may hold values from -1 to 1, as said below
Outputs:
- ritz_basis: float32 [64, 32, 32, 256], P(None, 'gz', 'gy', 'gx')
- projected: float32 [64, 64], replicated
Inputs may be any that keep to these rules, and one draw needn't show every extreme that they name: `bloch_sign`: each entry is -1 or +1.
All inputs are finite; a program needn't handle non-finite values.
Results may differ from a plain program's by a relative error of at most 0.00011.
Values sent between devices are 32-bit elements; how exact they have to be, the bound alone decides.
A program may use at most 128 MiB of HBM per device.

v0:
```python
import jax
import jax.numpy as jnp
from jax import lax
from jax.sharding import PartitionSpec as P

DEGREE = 6


def extended(block, sides, width):
    for axis, dim in sides:
        count = lax.axis_size(axis)
        forward = [(i, i + 1) for i in range(count - 1)]
        forward.append((count - 1, 0))
        backward = [(target, source) for source, target in forward]
        low = lax.ppermute(
            lax.slice_in_dim(block, block.shape[dim] - width, None, axis=dim), axis, forward
        )
        high = lax.ppermute(lax.slice_in_dim(block, 0, width, axis=dim), axis, backward)
        block = jnp.concatenate([low, block, high], axis=dim)
    return block


def lookup(phase_map, table):
    hits = phase_map[..., None] == jnp.arange(table.shape[0], dtype=jnp.int32)
    return jnp.sum(jnp.where(hits, table, jnp.float32(0.0)), axis=-1)


def gram(left, right):
    rows = left.shape[0]
    return jnp.dot(
        left.reshape(rows, -1), right.reshape(rows, -1).T, precision=lax.Precision.HIGHEST
    )


def stiffness(block, rho_pad, low_factor, high_factor):
    padded = extended(block, (("gx", 3), ("gy", 2), ("gz", 1)), 1)
    padded = padded.at[:, 0, 1:-1, 1:-1].multiply(low_factor[None])
    padded = padded.at[:, -1, 1:-1, 1:-1].multiply(high_factor[None])
    centre = padded[:, 1:-1, 1:-1, 1:-1]
    inv_rho = rho_pad[1:-1, 1:-1, 1:-1]
    w_up = 0.5 * (inv_rho + rho_pad[2:, 1:-1, 1:-1])
    w_down = 0.5 * (inv_rho + rho_pad[:-2, 1:-1, 1:-1])
    total = w_up * (centre - padded[:, 2:, 1:-1, 1:-1]) + w_down * (
        centre - padded[:, :-2, 1:-1, 1:-1]
    )
    w_up = 0.5 * (inv_rho + rho_pad[1:-1, 2:, 1:-1])
    w_down = 0.5 * (inv_rho + rho_pad[1:-1, :-2, 1:-1])
    total = total + (
        w_up * (centre - padded[:, 1:-1, 2:, 1:-1]) + w_down * (centre - padded[:, 1:-1, :-2, 1:-1])
    )
    w_up = 0.5 * (inv_rho + rho_pad[1:-1, 1:-1, 2:])
    w_down = 0.5 * (inv_rho + rho_pad[1:-1, 1:-1, :-2])
    total = total + (
        w_up * (centre - padded[:, 1:-1, 1:-1, 2:]) + w_down * (centre - padded[:, 1:-1, 1:-1, :-2])
    )
    return total


def body(initial_block, phase_map, phase_density, phase_modulus, bloch_sign):
    inv_rho = lookup(phase_map, 1.0 / phase_density)
    kappa = lookup(phase_map, phase_modulus)
    sign = bloch_sign.astype(jnp.float32)
    z_index = lax.axis_index("gz")
    z_count = lax.axis_size("gz")
    low_factor = jnp.where(z_index == 0, sign, jnp.float32(1.0))
    high_factor = jnp.where(z_index == z_count - 1, sign, jnp.float32(1.0))
    rho_pad = extended(inv_rho, (("gx", 2), ("gy", 1), ("gz", 0)), 1)
    top = 12.0 * jnp.max(phase_modulus) * jnp.max(1.0 / phase_density)
    low = 0.03 * top
    centre = (top + low) / 2.0
    half = (top - low) / 2.0
    cells = (
        initial_block.shape[1]
        * initial_block.shape[2]
        * initial_block.shape[3]
        * lax.axis_size("gx")
        * lax.axis_size("gy")
        * z_count
    )
    current = initial_block
    lap = kappa * stiffness(current, rho_pad, low_factor, high_factor)
    following = (lap - centre * current) / half
    previous, current = (current, following)
    for step in range(DEGREE - 1):
        lap = kappa * stiffness(current, rho_pad, low_factor, high_factor)
        following = 2.0 * (lap - centre * current) / half - previous
        previous, current = (current, following)
    correlation_local = gram(current / kappa[None], current)
    applied = stiffness(current, rho_pad, low_factor, high_factor)
    energy_local = gram(current, applied)
    correlation_total, energy_total = lax.psum(
        (correlation_local, energy_local), ("gx", "gy", "gz")
    )
    correlation = correlation_total / cells
    energy = energy_total / cells
    rows = current.shape[0]
    factor = jnp.linalg.cholesky(correlation)
    inverse = jax.scipy.linalg.solve_triangular(
        factor, jnp.eye(rows, dtype=jnp.float32), lower=True
    )
    basis = jnp.dot(inverse, current.reshape(rows, -1), precision=lax.Precision.HIGHEST).reshape(
        current.shape
    )
    projected = jnp.dot(
        jnp.dot(inverse, energy, precision=lax.Precision.HIGHEST),
        inverse.T,
        precision=lax.Precision.HIGHEST,
    )
    return (basis, projected)


def solution(mesh):
    in_specs = (P(None, "gz", "gy", "gx"), P("gz", "gy", "gx"), P(), P(), P("gy", "gx"))
    out_specs = (P(None, "gz", "gy", "gx"), P())
    return jax.shard_map(body, mesh=mesh, in_specs=in_specs, out_specs=out_specs, check_vma=False)
```

profile of v0, /device:TPU:0, one launch (start us, length us, event | category | flops | bytes accessed | tf_op | source)
XLA Modules:
  0.0 1980.2 jit_solution(10078879603563903501)
XLA Ops:
  88.8 86.9 %scatter-mul.46 = f32[64,10,10,130]{3,1,2,0:T(8,128)} dynamic-update-slice(f32[64,10,10,130]{3,1,2,0:T(8,128)} %pad_maximum_fusion, f32[64,1,8,128]{3,1,2,0:T(1,128)} %copy.195, s32[]{:T(128)} %constant.380.clone.1, s32[]{:T(128)} %constant.380.clone.1, s32[]{:T(128)} %constant.381.clone.1, s32[]{:T(128)} %constant.381.clone.1) | dynamic-update-slice | bytes 524292 | tf_op jit(solution)/shard_map/scatter-mul | solution.py:37
  178.5 87.5 %scatter-mul.49 = f32[64,10,10,130]{3,1,2,0:T(8,128)} dynamic-update-slice(f32[64,10,10,130]{3,1,2,0:T(8,128)} %scatter-mul.46, f32[64,1,8,128]{3,1,2,0:T(1,128)S(1)} %slice_multiply_fusion.12, s32[]{:T(128)} %constant.380.clone.1, s32[]{:T(128)} %constant.383.clone.1, s32[]{:T(128)} %constant.381.clone.1, s32[]{:T(128)} %constant.381.clone.1) | dynamic-update-slice | bytes 524292 | tf_op jit(solution)/shard_map/scatter-mul | solution.py:38
  266.0 19.6 fusion.96
  336.0 13.2 collective-permute-done.16
  357.8 87.4 %scatter-mul.50 = f32[64,10,10,130]{3,1,2,0:T(8,128)} dynamic-update-slice(f32[64,10,10,130]{3,1,2,0:T(8,128)} %pad_maximum_fusion.1, f32[64,1,8,128]{3,1,2,0:T(1,128)S(1)} %copy.211, s32[]{:T(128)} %constant.380.clone.1, s32[]{:T(128)} %constant.380.clone.1, s32[]{:T(128)} %constant.381.clone.1, s32[]{:T(128)} %constant.381.clone.1) | dynamic-update-slice | bytes 524292 | tf_op jit(solution)/shard_map/scatter-mul | solution.py:37
  448.1 87.5 %scatter-mul.51 = f32[64,10,10,130]{3,1,2,0:T(8,128)} dynamic-update-slice(f32[64,10,10,130]{3,1,2,0:T(8,128)} %scatter-mul.50, f32[64,1,8,128]{3,1,2,0:T(1,128)S(1)} %slice_multiply_fusion.10, s32[]{:T(128)} %constant.380.clone.1, s32[]{:T(128)} %constant.383.clone.1, s32[]{:T(128)} %constant.381.clone.1, s32[]{:T(128)} %constant.381.clone.1) | dynamic-update-slice | bytes 524292 | tf_op jit(solution)/shard_map/scatter-mul | solution.py:38
  535.6 20.8 %fusion.82 = f32[64,8,8,128]{3,1,2,0:T(8,128)} fusion(f32[64,10,10,130]{3,1,2,0:T(8,128)} %scatter-mul.51, f32[64,8,8,128]{3,1,2,0:T(8,128)S(1)} %fusion.96, f32[]{:T(128)S(6)} %div.58, f32[]{:T(128)S(6)} %div.57, f32[8,8,128]{2,0,1:T(8,128)S(1)} %copy.200, f32[8,8,128]{2,0,1:T(8,128)S(1)} %copy.199, f32[8,8,128]{2,0,1:T(8,128)S(1)} %copy.198, ...), kind=kLoop, calls=%fused_computation.121 | loop fusion | flops 12058624 | bytes 21200904 | tf_op jit(solution)/shard_map/sub | solution.py:86
  580.8 12.8 collective-permute-done.20
  608.2 13.2 collective-permute-done.22
  630.2 87.4 %scatter-mul.54 = f32[64,10,10,130]{3,1,2,0:T(8,128)} dynamic-update-slice(f32[64,10,10,130]{3,1,2,0:T(8,128)} %pad_maximum_fusion.2, f32[64,1,8,128]{3,1,2,0:T(1,128)S(1)} %copy.222, s32[]{:T(128)} %constant.380.clone.1, s32[]{:T(128)} %constant.380.clone.1, s32[]{:T(128)} %constant.381.clone.1, s32[]{:T(128)} %constant.381.clone.1) | dynamic-update-slice | bytes 524292 | tf_op jit(solution)/shard_map/scatter-mul | solution.py:37
  720.4 87.5 %scatter-mul.55 = f32[64,10,10,130]{3,1,2,0:T(8,128)} dynamic-update-slice(f32[64,10,10,130]{3,1,2,0:T(8,128)} %scatter-mul.54, f32[64,1,8,128]{3,1,2,0:T(1,128)S(1)} %slice_multiply_fusion.8, s32[]{:T(128)} %constant.380.clone.1, s32[]{:T(128)} %constant.383.clone.1, s32[]{:T(128)} %constant.381.clone.1, s32[]{:T(128)} %constant.381.clone.1) | dynamic-update-slice | bytes 524292 | tf_op jit(solution)/shard_map/scatter-mul | solution.py:38
  807.9 21.0 %fusion.66 = f32[64,8,8,128]{3,1,2,0:T(8,128)} fusion(f32[64,8,8,128]{3,1,2,0:T(8,128)S(1)} %fusion.96, f32[64,10,10,130]{3,1,2,0:T(8,128)} %scatter-mul.55, f32[64,8,8,128]{3,1,2,0:T(8,128)} %fusion.82, f32[]{:T(128)S(6)} %div.58, f32[]{:T(128)S(6)} %div.57, f32[8,8,128]{2,0,1:T(8,128)S(1)} %copy.200, f32[8,8,128]{2,0,1:T(8,128)S(1)} %copy.199, ...), kind=kLoop, calls=%fused_computation.99 | loop fusion | flops 12058624 | bytes 21200904 | tf_op jit(solution)/shard_map/sub | solution.py:86
  851.4 12.8 collective-permute-done.26
  879.6 13.5 collective-permute-done.28
  902.1 87.4 %scatter-mul.56 = f32[64,10,10,130]{3,1,2,0:T(8,128)} dynamic-update-slice(f32[64,10,10,130]{3,1,2,0:T(8,128)} %pad_maximum_fusion.3, f32[64,1,8,128]{3,1,2,0:T(1,128)S(1)} %copy.232, s32[]{:T(128)} %constant.380.clone.1, s32[]{:T(128)} %constant.380.clone.1, s32[]{:T(128)} %constant.381.clone.1, s32[]{:T(128)} %constant.381.clone.1) | dynamic-update-slice | bytes 524292 | tf_op jit(solution)/shard_map/scatter-mul | solution.py:37
  992.4 87.5 %scatter-mul.59 = f32[64,10,10,130]{3,1,2,0:T(8,128)} dynamic-update-slice(f32[64,10,10,130]{3,1,2,0:T(8,128)} %scatter-mul.56, f32[64,1,8,128]{3,1,2,0:T(1,128)S(1)} %slice_multiply_fusion.6, s32[]{:T(128)} %constant.380.clone.1, s32[]{:T(128)} %constant.383.clone.1, s32[]{:T(128)} %constant.381.clone.1, s32[]{:T(128)} %constant.381.clone.1) | dynamic-update-slice | bytes 524292 | tf_op jit(solution)/shard_map/scatter-mul | solution.py:38
  1079.9 20.8 %fusion.50 = f32[64,8,8,128]{3,1,2,0:T(8,128)S(1)} fusion(f32[64,8,8,128]{3,1,2,0:T(8,128)} %fusion.82, f32[64,10,10,130]{3,1,2,0:T(8,128)} %scatter-mul.59, f32[64,8,8,128]{3,1,2,0:T(8,128)} %fusion.66, f32[]{:T(128)S(6)} %div.58, f32[]{:T(128)S(6)} %div.57, f32[8,8,128]{2,0,1:T(8,128)S(1)} %copy.200, f32[8,8,128]{2,0,1:T(8,128)S(1)} %copy.199, ...), kind=kLoop, calls=%fused_computation.77 | loop fusion | flops 12058624 | bytes 21200904 | tf_op jit(solution)/shard_map/sub | solution.py:86
  1122.8 12.8 collective-permute-done.32
  1150.7 13.5 collective-permute-done.34
  1173.0 87.4 %scatter-mul.60 = f32[64,10,10,130]{3,1,2,0:T(8,128)} dynamic-update-slice(f32[64,10,10,130]{3,1,2,0:T(8,128)} %pad_maximum_fusion.4, f32[64,1,8,128]{3,1,2,0:T(1,128)S(1)} %copy.242, s32[]{:T(128)} %constant.380.clone.1, s32[]{:T(128)} %constant.380.clone.1, s32[]{:T(128)} %constant.381.clone.1, s32[]{:T(128)} %constant.381.clone.1) | dynamic-update-slice | bytes 524292 | tf_op jit(solution)/shard_map/scatter-mul | solution.py:37
  1263.3 87.5 %scatter-mul.61 = f32[64,10,10,130]{3,1,2,0:T(8,128)} dynamic-update-slice(f32[64,10,10,130]{3,1,2,0:T(8,128)} %scatter-mul.60, f32[64,1,8,128]{3,1,2,0:T(1,128)S(1)} %slice_multiply_fusion.4, s32[]{:T(128)} %constant.380.clone.1, s32[]{:T(128)} %constant.383.clone.1, s32[]{:T(128)} %constant.381.clone.1, s32[]{:T(128)} %constant.381.clone.1) | dynamic-update-slice | bytes 524292 | tf_op jit(solution)/shard_map/scatter-mul | solution.py:38
  1350.8 20.6 %fusion.34 = f32[64,8,8,128]{3,1,2,0:T(8,128)} fusion(f32[64,8,8,128]{3,1,2,0:T(8,128)} %fusion.66, f32[64,10,10,130]{3,1,2,0:T(8,128)} %scatter-mul.61, f32[64,8,8,128]{3,1,2,0:T(8,128)S(1)} %fusion.50, f32[]{:T(128)S(6)} %div.58, f32[]{:T(128)S(6)} %div.57, f32[8,8,128]{2,0,1:T(8,128)S(1)} %copy.200, f32[8,8,128]{2,0,1:T(8,128)S(1)} %copy.199, ...), kind=kLoop, calls=%fused_computation.55 | loop fusion | flops 12058624 | bytes 21200904 | tf_op jit(solution)/shard_map/sub | solution.py:86
  1393.9 12.8 collective-permute-done.38
  1420.9 13.5 collective-permute-done.40
  1443.5 87.4 %scatter-mul.64 = f32[64,10,10,130]{3,1,2,0:T(8,128)} dynamic-update-slice(f32[64,10,10,130]{3,1,2,0:T(8,128)} %pad_maximum_fusion.5, f32[64,1,8,128]{3,1,2,0:T(1,128)S(1)} %copy.252, s32[]{:T(128)} %constant.380.clone.1, s32[]{:T(128)} %constant.380.clone.1, s32[]{:T(128)} %constant.381.clone.1, s32[]{:T(128)} %constant.381.clone.1) | dynamic-update-slice | bytes 524292 | tf_op jit(solution)/shard_map/scatter-mul | solution.py:37
  1533.7 87.5 %scatter-mul.65 = f32[64,10,10,130]{3,1,2,0:T(8,128)} dynamic-update-slice(f32[64,10,10,130]{3,1,2,0:T(8,128)} %scatter-mul.64, f32[64,1,8,128]{3,1,2,0:T(1,128)S(1)} %slice_multiply_fusion.2, s32[]{:T(128)} %constant.380.clone.1, s32[]{:T(128)} %constant.383.clone.1, s32[]{:T(128)} %constant.381.clone.1, s32[]{:T(128)} %constant.381.clone.1) | dynamic-update-slice | bytes 524292 | tf_op jit(solution)/shard_map/scatter-mul | solution.py:38
  1621.2 21.8 %broadcast_divide_fusion = (f32[64,8,8,128]{3,1,2,0:T(8,128)}, f32[64,8,8,128]{3,1,2,0:T(8,128)S(1)}) fusion(f32[8,8,128]{2,0,1:T(8,128)S(1)} %copy.183, f32[64,8,8,128]{3,1,2,0:T(8,128)} %copy-done, f32[]{:T(128)S(6)} %div.58, f32[64,8,8,128]{3,1,2,0:T(8,128)} %fusion.34, f32[]{:T(128)S(6)} %div.57, f32[64,10,10,130]{3,1,2,0:T(8,128)} %scatter-mul.65, ...), kind=kLoop, calls=%fused_computation.165 | loop fusion | flops 12582912 | bytes 23298056 | tf_op jit(solution)/shard_map/div | solution.py:88
  1665.0 12.9 collective-permute-done.44
  1714.9 87.4 %scatter-mul.66 = f32[64,10,10,130]{3,1,2,0:T(8,128)} dynamic-update-slice(f32[64,10,10,130]{3,1,2,0:T(8,128)} %pad_maximum_fusion.6, f32[64,1,8,128]{3,1,2,0:T(1,128)S(1)} %copy.268, s32[]{:T(128)} %constant.380.clone.1, s32[]{:T(128)} %constant.380.clone.1, s32[]{:T(128)} %constant.381.clone.1, s32[]{:T(128)} %constant.381.clone.1) | dynamic-update-slice | bytes 524292 | tf_op jit(solution)/shard_map/scatter-mul | solution.py:37
  1805.2 87.5 %scatter-mul.69 = f32[64,10,10,130]{3,1,2,0:T(8,128)} dynamic-update-slice(f32[64,10,10,130]{3,1,2,0:T(8,128)} %scatter-mul.66, f32[64,1,8,128]{3,1,2,0:T(1,128)S(1)} %slice_multiply_fusion, s32[]{:T(128)} %constant.380.clone.1, s32[]{:T(128)} %constant.383.clone.1, s32[]{:T(128)} %constant.381.clone.1, s32[]{:T(128)} %constant.381.clone.1) | dynamic-update-slice | bytes 524292 | tf_op jit(solution)/shard_map/scatter-mul | solution.py:38
  1892.6 19.9 %fusion.2 = f32[64,8,8,128]{3,1,2,0:T(8,128)} fusion(f32[64,10,10,130]{3,1,2,0:T(8,128)} %scatter-mul.69, f32[8,8,128]{2,0,1:T(8,128)S(1)} %copy.200, f32[8,8,128]{2,0,1:T(8,128)S(1)} %copy.199, f32[8,8,128]{2,0,1:T(8,128)S(1)} %copy.198, f32[8,8,128]{2,0,1:T(8,128)S(1)} %copy.197, f32[8,8,128]{2,0,1:T(8,128)S(1)} %copy.196, f32[8,8,128]{2,0,1:T(8,128)S(1)} %copy.184), kind=kLoop, calls=%fused_computation.11 | loop fusion | flops 8912896 | bytes 16973824 | tf_op jit(solution)/shard_map/add | solution.py:53
  1918.2 41.0 %all-reduce = (f32[64,64]{0,1:T(8,128)S(1)}, f32[64,64]{0,1:T(8,128)S(1)}) all-reduce(f32[64,64]{0,1:T(8,128)S(1)} %fusion.113, f32[64,64]{0,1:T(8,128)S(1)} %fusion.118), channel_id=1, replica_groups=mesh['gx'=2,'gy'=4,'gz'=4] {'gx','gy','gz'}, use_global_device_ids=true, to_apply=%region_4.5 | all-reduce | flops 8192 | bytes 65536 | tf_op jit(solution)/shard_map/psum | solution.py:91
  (272 shorter events, 436.3 us)
Async XLA Ops:
  2.8 17.3 collective-permute-start.1
  20.3 18.4 collective-permute-start.3
  32.9 16.9 collective-permute-start.7
  32.9 23.7 %collective-permute-start.8 = (f32[64,8,1,130]{3,1,2,0:T(8,128)}, f32[64,8,1,130]{3,1,2,0:T(8,128)S(1)}, u32[]{:S(2)}, u32[]{:S(2)}) collective-permute-start(f32[64,8,1,130]{3,1,2,0:T(8,128)} %get-tuple-element.215), channel_id=1, source_target_pairs={{4,0},{8,4},{12,8},{0,12},{5,1},{9,5},{13,9},{1,13},{6,2},{10,6},{... | collective-permute-start | bytes 798728 | tf_op jit(solution)/shard_map/ppermute | solution.py:18
  38.8 27.7 %collective-permute-start.4 = (f32[1,10,130]{2,1,0:T(8,128)S(1)}, f32[1,10,130]{2,1,0:T(8,128)S(1)}, u32[]{:S(2)}, u32[]{:S(2)}) collective-permute-start(f32[1,10,130]{2,1,0:T(8,128)S(1)} %get-tuple-element.232), channel_id=1, source_target_pairs={{1,0},{2,1},{3,2},{0,3},{5,4},{6,5},{7,6},{4,7},{9,8},{10,9},{11,1... | collective-permute-start | bytes 15608 | tf_op jit(solution)/shard_map/ppermute | solution.py:18
  38.8 27.7 %collective-permute-start.11 = (f32[1,10,130]{2,1,0:T(8,128)S(1)}, f32[1,10,130]{2,1,0:T(8,128)S(1)}, u32[]{:S(2)}, u32[]{:S(2)}) collective-permute-start(f32[1,10,130]{2,1,0:T(8,128)S(1)} %get-tuple-element.233), channel_id=1, source_target_pairs={{0,1},{1,2},{2,3},{3,0},{4,5},{5,6},{6,7},{7,4},{8,9},{9,10},{10,1... | collective-permute-start | bytes 15608 | tf_op jit(solution)/shard_map/ppermute | solution.py:15
  64.4 14.9 collective-permute-start.9
  64.7 16.4 collective-permute-start.10
  303.7 16.8 collective-permute-start.14
  306.1 23.7 %collective-permute-start.15 = (f32[64,8,1,130]{3,1,2,0:T(8,128)S(1)}, f32[64,8,1,130]{3,1,2,0:T(8,128)S(1)}, u32[]{:S(2)}, u32[]{:S(2)}) collective-permute-start(f32[64,8,1,130]{3,1,2,0:T(8,128)S(1)} %get-tuple-element.213), channel_id=1, source_target_pairs={{4,0},{8,4},{12,8},{0,12},{5,1},{9,5},{13,9},{1,13},{6,2},{10,6},{... | collective-permute-start | bytes 798728 | tf_op jit(solution)/shard_map/ppermute | solution.py:18
  334.1 15.1 collective-permute-start.16
  334.2 16.1 collective-permute-start.17
  576.9 16.7 collective-permute-start.20
  577.5 24.4 %collective-permute-start.21 = (f32[64,8,1,130]{3,1,2,0:T(8,128)S(1)}, f32[64,8,1,130]{3,1,2,0:T(8,128)S(1)}, u32[]{:S(2)}, u32[]{:S(2)}) collective-permute-start(f32[64,8,1,130]{3,1,2,0:T(8,128)S(1)} %get-tuple-element.211), channel_id=1, source_target_pairs={{4,0},{8,4},{12,8},{0,12},{5,1},{9,5},{13,9},{1,13},{6,2},{10,6},{... | collective-permute-start | bytes 798728 | tf_op jit(solution)/shard_map/ppermute | solution.py:18
  606.3 15.1 collective-permute-start.22
  606.4 16.1 collective-permute-start.23
  847.5 16.7 collective-permute-start.26
  848.8 24.6 %collective-permute-start.27 = (f32[64,8,1,130]{3,1,2,0:T(8,128)S(1)}, f32[64,8,1,130]{3,1,2,0:T(8,128)S(1)}, u32[]{:S(2)}, u32[]{:S(2)}) collective-permute-start(f32[64,8,1,130]{3,1,2,0:T(8,128)S(1)} %get-tuple-element.209), channel_id=1, source_target_pairs={{4,0},{8,4},{12,8},{0,12},{5,1},{9,5},{13,9},{1,13},{6,2},{10,6},{... | collective-permute-start | bytes 798728 | tf_op jit(solution)/shard_map/ppermute | solution.py:18
  877.6 15.4 collective-permute-start.28
  877.8 16.4 collective-permute-start.29
  1118.9 16.7 collective-permute-start.32
  1120.4 24.1 %collective-permute-start.33 = (f32[64,8,1,130]{3,1,2,0:T(8,128)S(1)}, f32[64,8,1,130]{3,1,2,0:T(8,128)S(1)}, u32[]{:S(2)}, u32[]{:S(2)}) collective-permute-start(f32[64,8,1,130]{3,1,2,0:T(8,128)S(1)} %get-tuple-element.207), channel_id=1, source_target_pairs={{4,0},{8,4},{12,8},{0,12},{5,1},{9,5},{13,9},{1,13},{6,2},{10,6},{... | collective-permute-start | bytes 798728 | tf_op jit(solution)/shard_map/ppermute | solution.py:18
  1148.8 15.4 collective-permute-start.34
  1148.9 16.4 collective-permute-start.35
  1390.0 16.7 collective-permute-start.38
  1390.7 24.0 %collective-permute-start.39 = (f32[64,8,1,130]{3,1,2,0:T(8,128)S(1)}, f32[64,8,1,130]{3,1,2,0:T(8,128)S(1)}, u32[]{:S(2)}, u32[]{:S(2)}) collective-permute-start(f32[64,8,1,130]{3,1,2,0:T(8,128)S(1)} %get-tuple-element.205), channel_id=1, source_target_pairs={{4,0},{8,4},{12,8},{0,12},{5,1},{9,5},{13,9},{1,13},{6,2},{10,6},{... | collective-permute-start | bytes 798728 | tf_op jit(solution)/shard_map/ppermute | solution.py:18
  1419.0 15.4 collective-permute-start.40
  1419.1 16.4 collective-permute-start.41
  1661.2 16.7 collective-permute-start.44
  1662.4 24.1 %collective-permute-start.45 = (f32[64,8,1,130]{3,1,2,0:T(8,128)S(1)}, f32[64,8,1,130]{3,1,2,0:T(8,128)S(1)}, u32[]{:S(2)}, u32[]{:S(2)}) collective-permute-start(f32[64,8,1,130]{3,1,2,0:T(8,128)S(1)} %get-tuple-element.203), channel_id=1, source_target_pairs={{4,0},{8,4},{12,8},{0,12},{5,1},{9,5},{13,9},{1,13},{6,2},{10,6},{... | collective-permute-start | bytes 798728 | tf_op jit(solution)/shard_map/ppermute | solution.py:18
  1690.8 15.2 collective-permute-start.46
  1690.9 16.2 collective-permute-start.47
  (39 other events, 780.6 us)
where the time goes:
time: 1990 us; the launch traced here: 1980 us
  local copies, waits for them, and re-layouts  1350 us (68%)
  other arithmetic  277 us (14%)
  waiting for transfers between devices  234 us (12%)
  starting transfers between devices  62.9 us (3%)
  blocking collectives  41 us (2%)
    another operation x7, local copies, waits for them, and re-layouts, stiffness(): padded = padded.at[:, -1, 1:-1, 1:-1].multiply(high_factor[None])  612 us
    another operation x7, local copies, waits for them, and re-layouts, stiffness(): padded = padded.at[:, 0, 1:-1, 1:-1].multiply(low_factor[None])  612 us
    ppermute x24, waiting for transfers between devices, extended(): lax.ppermute(lax.slice_in_dim(block, block.shape[dim] - width, None, axis...  173 us
    sub x4, other arithmetic, body(): following = 2.0 * (lap - centre * current) / half - previous  83.2 us
    ppermute x24, waiting for transfers between devices, extended(): lax.ppermute(lax.slice_in_dim(block, 0, width, axis=dim), axis, backward)  61 us
    concatenate x8, other arithmetic, extended(): block = jnp.concatenate([low, block, high], axis=dim)  49.4 us
    slice x14, other arithmetic, extended(): lax.slice_in_dim(block, block.shape[dim] - width, None, axis=dim)  46.8 us
    ppermute x24, starting transfers between devices, extended(): lax.ppermute(lax.slice_in_dim(block, 0, width, axis=dim), axis, backward)  45 us
  transfers between devices with their start and end apart: 48, of which 27 were waited for; matrix products, arithmetic and copies ran while one was open for 4% of the time, Pallas kernels for 0%

commit v1 on v0

--- a/solution.py
+++ b/solution.py
@@ -89,7 +89,7 @@
     applied = stiffness(current, rho_pad, low_factor, high_factor)
     energy_local = gram(current, applied)
     correlation_total, energy_total = lax.psum(
-        (correlation_local, energy_local), ("gx", "gy", "gz")
+        lax.psum((correlation_local, energy_local), ("gy", "gz")), "gx"
     )
     correlation = correlation_total / cells
     energy = energy_total / cells

time: 1990 us -> 2010 us (1.010)
  blocking collectives: 41 us -> 69.6 us
    psum x1 -> x2, blocking collectives: 41 us -> 69.6 us  [the longest x1 60.5 us: body(): lax.psum((correlation_local, energy_local), ('gy', 'gz'))]
where the time goes in v1:
time: 2010 us; the launch traced here: 2000 us
  local copies, waits for them, and re-layouts  1350 us (67%)
  other arithmetic  272 us (14%)
  waiting for transfers between devices  234 us (12%)
  blocking collectives  69.6 us (3%)
  starting transfers between devices  62.9 us (3%)
    another operation x7, local copies, waits for them, and re-layouts, stiffness(): padded = padded.at[:, -1, 1:-1, 1:-1].multiply(high_factor[None])  612 us
    another operation x7, local copies, waits for them, and re-layouts, stiffness(): padded = padded.at[:, 0, 1:-1, 1:-1].multiply(low_factor[None])  612 us
    ppermute x24, waiting for transfers between devices, extended(): lax.ppermute(lax.slice_in_dim(block, block.shape[dim] - width, None, axis...  173 us
    sub x4, other arithmetic, body(): following = 2.0 * (lap - centre * current) / half - previous  80.8 us
    ppermute x24, waiting for transfers between devices, extended(): lax.ppermute(lax.slice_in_dim(block, 0, width, axis=dim), axis, backward)  61 us
    psum x1, blocking collectives, body(): lax.psum((correlation_local, energy_local), ('gy', 'gz'))  60.5 us
    concatenate x8, other arithmetic, extended(): block = jnp.concatenate([low, block, high], axis=dim)  49.3 us
    slice x14, other arithmetic, extended(): lax.slice_in_dim(block, block.shape[dim] - width, None, axis=dim)  46.7 us
  transfers between devices with their start and end apart: 48, of which 27 were waited for; matrix products, arithmetic and copies ran while one was open for 4% of the time, Pallas kernels for 0%

profile of v1, /device:TPU:0, one launch (start us, length us, event | category | flops | bytes accessed | tf_op | source)
XLA Modules:
  0.0 2004.5 jit_solution(6943103890492906240)
XLA Ops:
  88.7 86.9 %scatter-mul.46 = f32[64,10,10,130]{3,1,2,0:T(8,128)} dynamic-update-slice(f32[64,10,10,130]{3,1,2,0:T(8,128)} %pad_maximum_fusion, f32[64,1,8,128]{3,1,2,0:T(1,128)} %copy.195, s32[]{:T(128)} %constant.380.clone.1, s32[]{:T(128)} %constant.380.clone.1, s32[]{:T(128)} %constant.381.clone.1, s32[]{:T(128)} %constant.381.clone.1) | dynamic-update-slice | bytes 524292 | tf_op jit(solution)/shard_map/scatter-mul | solution.py:37
  178.5 87.5 %scatter-mul.49 = f32[64,10,10,130]{3,1,2,0:T(8,128)} dynamic-update-slice(f32[64,10,10,130]{3,1,2,0:T(8,128)} %scatter-mul.46, f32[64,1,8,128]{3,1,2,0:T(1,128)S(1)} %slice_multiply_fusion.12, s32[]{:T(128)} %constant.380.clone.1, s32[]{:T(128)} %constant.383.clone.1, s32[]{:T(128)} %constant.381.clone.1, s32[]{:T(128)} %constant.381.clone.1) | dynamic-update-slice | bytes 524292 | tf_op jit(solution)/shard_map/scatter-mul | solution.py:38
  266.0 19.0 fusion.96
  335.4 13.2 collective-permute-done.16
  357.2 87.4 %scatter-mul.50 = f32[64,10,10,130]{3,1,2,0:T(8,128)} dynamic-update-slice(f32[64,10,10,130]{3,1,2,0:T(8,128)} %pad_maximum_fusion.1, f32[64,1,8,128]{3,1,2,0:T(1,128)S(1)} %copy.211, s32[]{:T(128)} %constant.380.clone.1, s32[]{:T(128)} %constant.380.clone.1, s32[]{:T(128)} %constant.381.clone.1, s32[]{:T(128)} %constant.381.clone.1) | dynamic-update-slice | bytes 524292 | tf_op jit(solution)/shard_map/scatter-mul | solution.py:37
  447.5 87.5 %scatter-mul.51 = f32[64,10,10,130]{3,1,2,0:T(8,128)} dynamic-update-slice(f32[64,10,10,130]{3,1,2,0:T(8,128)} %scatter-mul.50, f32[64,1,8,128]{3,1,2,0:T(1,128)S(1)} %slice_multiply_fusion.10, s32[]{:T(128)} %constant.380.clone.1, s32[]{:T(128)} %constant.383.clone.1, s32[]{:T(128)} %constant.381.clone.1, s32[]{:T(128)} %constant.381.clone.1) | dynamic-update-slice | bytes 524292 | tf_op jit(solution)/shard_map/scatter-mul | solution.py:38
  534.9 20.2 %fusion.82 = f32[64,8,8,128]{3,1,2,0:T(8,128)} fusion(f32[64,10,10,130]{3,1,2,0:T(8,128)} %scatter-mul.51, f32[64,8,8,128]{3,1,2,0:T(8,128)S(1)} %fusion.96, f32[]{:T(128)S(6)} %div.58, f32[]{:T(128)S(6)} %div.57, f32[8,8,128]{2,0,1:T(8,128)S(1)} %copy.200, f32[8,8,128]{2,0,1:T(8,128)S(1)} %copy.199, f32[8,8,128]{2,0,1:T(8,128)S(1)} %copy.198, ...), kind=kLoop, calls=%fused_computation.121 | loop fusion | flops 12058624 | bytes 21200904 | tf_op jit(solution)/shard_map/sub | solution.py:86
  579.6 12.8 collective-permute-done.20
  607.0 13.2 collective-permute-done.22
  629.0 87.4 %scatter-mul.54 = f32[64,10,10,130]{3,1,2,0:T(8,128)} dynamic-update-slice(f32[64,10,10,130]{3,1,2,0:T(8,128)} %pad_maximum_fusion.2, f32[64,1,8,128]{3,1,2,0:T(1,128)S(1)} %copy.222, s32[]{:T(128)} %constant.380.clone.1, s32[]{:T(128)} %constant.380.clone.1, s32[]{:T(128)} %constant.381.clone.1, s32[]{:T(128)} %constant.381.clone.1) | dynamic-update-slice | bytes 524292 | tf_op jit(solution)/shard_map/scatter-mul | solution.py:37
  719.3 87.5 %scatter-mul.55 = f32[64,10,10,130]{3,1,2,0:T(8,128)} dynamic-update-slice(f32[64,10,10,130]{3,1,2,0:T(8,128)} %scatter-mul.54, f32[64,1,8,128]{3,1,2,0:T(1,128)S(1)} %slice_multiply_fusion.8, s32[]{:T(128)} %constant.380.clone.1, s32[]{:T(128)} %constant.383.clone.1, s32[]{:T(128)} %constant.381.clone.1, s32[]{:T(128)} %constant.381.clone.1) | dynamic-update-slice | bytes 524292 | tf_op jit(solution)/shard_map/scatter-mul | solution.py:38
  806.8 20.3 %fusion.66 = f32[64,8,8,128]{3,1,2,0:T(8,128)} fusion(f32[64,8,8,128]{3,1,2,0:T(8,128)S(1)} %fusion.96, f32[64,10,10,130]{3,1,2,0:T(8,128)} %scatter-mul.55, f32[64,8,8,128]{3,1,2,0:T(8,128)} %fusion.82, f32[]{:T(128)S(6)} %div.58, f32[]{:T(128)S(6)} %div.57, f32[8,8,128]{2,0,1:T(8,128)S(1)} %copy.200, f32[8,8,128]{2,0,1:T(8,128)S(1)} %copy.199, ...), kind=kLoop, calls=%fused_computation.99 | loop fusion | flops 12058624 | bytes 21200904 | tf_op jit(solution)/shard_map/sub | solution.py:86
  849.6 12.8 collective-permute-done.26
  877.8 13.5 collective-permute-done.28
  900.3 87.4 %scatter-mul.56 = f32[64,10,10,130]{3,1,2,0:T(8,128)} dynamic-update-slice(f32[64,10,10,130]{3,1,2,0:T(8,128)} %pad_maximum_fusion.3, f32[64,1,8,128]{3,1,2,0:T(1,128)S(1)} %copy.232, s32[]{:T(128)} %constant.380.clone.1, s32[]{:T(128)} %constant.380.clone.1, s32[]{:T(128)} %constant.381.clone.1, s32[]{:T(128)} %constant.381.clone.1) | dynamic-update-slice | bytes 524292 | tf_op jit(solution)/shard_map/scatter-mul | solution.py:37
  990.6 87.5 %scatter-mul.59 = f32[64,10,10,130]{3,1,2,0:T(8,128)} dynamic-update-slice(f32[64,10,10,130]{3,1,2,0:T(8,128)} %scatter-mul.56, f32[64,1,8,128]{3,1,2,0:T(1,128)S(1)} %slice_multiply_fusion.6, s32[]{:T(128)} %constant.380.clone.1, s32[]{:T(128)} %constant.383.clone.1, s32[]{:T(128)} %constant.381.clone.1, s32[]{:T(128)} %constant.381.clone.1) | dynamic-update-slice | bytes 524292 | tf_op jit(solution)/shard_map/scatter-mul | solution.py:38
  1078.1 20.1 %fusion.50 = f32[64,8,8,128]{3,1,2,0:T(8,128)S(1)} fusion(f32[64,8,8,128]{3,1,2,0:T(8,128)} %fusion.82, f32[64,10,10,130]{3,1,2,0:T(8,128)} %scatter-mul.59, f32[64,8,8,128]{3,1,2,0:T(8,128)} %fusion.66, f32[]{:T(128)S(6)} %div.58, f32[]{:T(128)S(6)} %div.57, f32[8,8,128]{2,0,1:T(8,128)S(1)} %copy.200, f32[8,8,128]{2,0,1:T(8,128)S(1)} %copy.199, ...), kind=kLoop, calls=%fused_computation.77 | loop fusion | flops 12058624 | bytes 21200904 | tf_op jit(solution)/shard_map/sub | solution.py:86
  1120.3 12.8 collective-permute-done.32
  1148.3 13.5 collective-permute-done.34
  1170.6 87.4 %scatter-mul.60 = f32[64,10,10,130]{3,1,2,0:T(8,128)} dynamic-update-slice(f32[64,10,10,130]{3,1,2,0:T(8,128)} %pad_maximum_fusion.4, f32[64,1,8,128]{3,1,2,0:T(1,128)S(1)} %copy.242, s32[]{:T(128)} %constant.380.clone.1, s32[]{:T(128)} %constant.380.clone.1, s32[]{:T(128)} %constant.381.clone.1, s32[]{:T(128)} %constant.381.clone.1) | dynamic-update-slice | bytes 524292 | tf_op jit(solution)/shard_map/scatter-mul | solution.py:37
  1260.8 87.5 %scatter-mul.61 = f32[64,10,10,130]{3,1,2,0:T(8,128)} dynamic-update-slice(f32[64,10,10,130]{3,1,2,0:T(8,128)} %scatter-mul.60, f32[64,1,8,128]{3,1,2,0:T(1,128)S(1)} %slice_multiply_fusion.4, s32[]{:T(128)} %constant.380.clone.1, s32[]{:T(128)} %constant.383.clone.1, s32[]{:T(128)} %constant.381.clone.1, s32[]{:T(128)} %constant.381.clone.1) | dynamic-update-slice | bytes 524292 | tf_op jit(solution)/shard_map/scatter-mul | solution.py:38
  1348.3 20.1 %fusion.34 = f32[64,8,8,128]{3,1,2,0:T(8,128)} fusion(f32[64,8,8,128]{3,1,2,0:T(8,128)} %fusion.66, f32[64,10,10,130]{3,1,2,0:T(8,128)} %scatter-mul.61, f32[64,8,8,128]{3,1,2,0:T(8,128)S(1)} %fusion.50, f32[]{:T(128)S(6)} %div.58, f32[]{:T(128)S(6)} %div.57, f32[8,8,128]{2,0,1:T(8,128)S(1)} %copy.200, f32[8,8,128]{2,0,1:T(8,128)S(1)} %copy.199, ...), kind=kLoop, calls=%fused_computation.55 | loop fusion | flops 12058624 | bytes 21200904 | tf_op jit(solution)/shard_map/sub | solution.py:86
  1390.9 12.8 collective-permute-done.38
  1417.9 13.5 collective-permute-done.40
  1440.5 87.4 %scatter-mul.64 = f32[64,10,10,130]{3,1,2,0:T(8,128)} dynamic-update-slice(f32[64,10,10,130]{3,1,2,0:T(8,128)} %pad_maximum_fusion.5, f32[64,1,8,128]{3,1,2,0:T(1,128)S(1)} %copy.252, s32[]{:T(128)} %constant.380.clone.1, s32[]{:T(128)} %constant.380.clone.1, s32[]{:T(128)} %constant.381.clone.1, s32[]{:T(128)} %constant.381.clone.1) | dynamic-update-slice | bytes 524292 | tf_op jit(solution)/shard_map/scatter-mul | solution.py:37
  1530.8 87.5 %scatter-mul.65 = f32[64,10,10,130]{3,1,2,0:T(8,128)} dynamic-update-slice(f32[64,10,10,130]{3,1,2,0:T(8,128)} %scatter-mul.64, f32[64,1,8,128]{3,1,2,0:T(1,128)S(1)} %slice_multiply_fusion.2, s32[]{:T(128)} %constant.380.clone.1, s32[]{:T(128)} %constant.383.clone.1, s32[]{:T(128)} %constant.381.clone.1, s32[]{:T(128)} %constant.381.clone.1) | dynamic-update-slice | bytes 524292 | tf_op jit(solution)/shard_map/scatter-mul | solution.py:38
  1618.2 21.1 %broadcast_divide_fusion = (f32[64,8,8,128]{3,1,2,0:T(8,128)}, f32[64,8,8,128]{3,1,2,0:T(8,128)S(1)}) fusion(f32[8,8,128]{2,0,1:T(8,128)S(1)} %copy.183, f32[64,8,8,128]{3,1,2,0:T(8,128)} %copy-done, f32[]{:T(128)S(6)} %div.58, f32[64,8,8,128]{3,1,2,0:T(8,128)} %fusion.34, f32[]{:T(128)S(6)} %div.57, f32[64,10,10,130]{3,1,2,0:T(8,128)} %scatter-mul.65, ...), kind=kLoop, calls=%fused_computation.165 | loop fusion | flops 12582912 | bytes 23298056 | tf_op jit(solution)/shard_map/div | solution.py:88
  1661.4 12.9 collective-permute-done.44
  1711.3 87.4 %scatter-mul.66 = f32[64,10,10,130]{3,1,2,0:T(8,128)} dynamic-update-slice(f32[64,10,10,130]{3,1,2,0:T(8,128)} %pad_maximum_fusion.6, f32[64,1,8,128]{3,1,2,0:T(1,128)S(1)} %copy.268, s32[]{:T(128)} %constant.380.clone.1, s32[]{:T(128)} %constant.380.clone.1, s32[]{:T(128)} %constant.381.clone.1, s32[]{:T(128)} %constant.381.clone.1) | dynamic-update-slice | bytes 524292 | tf_op jit(solution)/shard_map/scatter-mul | solution.py:37
  1801.6 87.5 %scatter-mul.69 = f32[64,10,10,130]{3,1,2,0:T(8,128)} dynamic-update-slice(f32[64,10,10,130]{3,1,2,0:T(8,128)} %scatter-mul.66, f32[64,1,8,128]{3,1,2,0:T(1,128)S(1)} %slice_multiply_fusion, s32[]{:T(128)} %constant.380.clone.1, s32[]{:T(128)} %constant.383.clone.1, s32[]{:T(128)} %constant.381.clone.1, s32[]{:T(128)} %constant.381.clone.1) | dynamic-update-slice | bytes 524292 | tf_op jit(solution)/shard_map/scatter-mul | solution.py:38
  1889.0 19.3 fusion.2
  1913.9 60.5 %all-reduce = (f32[64,64]{0,1:T(8,128)S(1)}, f32[64,64]{0,1:T(8,128)S(1)}) all-reduce(f32[64,64]{0,1:T(8,128)S(1)} %fusion.113, f32[64,64]{0,1:T(8,128)S(1)} %fusion.118), channel_id=1, replica_groups=mesh['gx'=2,'gy'=4,'gz'=4] {'gy','gz'}, use_global_device_ids=true, to_apply=%region_4.5 | all-reduce | flops 8192 | bytes 65536 | tf_op jit(solution)/shard_map/psum | solution.py:92
  (273 shorter events, 445.5 us)
Async XLA Ops:
  2.8 17.3 collective-permute-start.1
  20.3 18.3 collective-permute-start.3
  32.9 16.9 collective-permute-start.7
  32.9 23.7 %collective-permute-start.8 = (f32[64,8,1,130]{3,1,2,0:T(8,128)}, f32[64,8,1,130]{3,1,2,0:T(8,128)S(1)}, u32[]{:S(2)}, u32[]{:S(2)}) collective-permute-start(f32[64,8,1,130]{3,1,2,0:T(8,128)} %get-tuple-element.217), channel_id=1, source_target_pairs={{4,0},{8,4},{12,8},{0,12},{5,1},{9,5},{13,9},{1,13},{6,2},{10,6},{... | collective-permute-start | bytes 798728 | tf_op jit(solution)/shard_map/ppermute | solution.py:18
  38.7 27.8 %collective-permute-start.4 = (f32[1,10,130]{2,1,0:T(8,128)S(1)}, f32[1,10,130]{2,1,0:T(8,128)S(1)}, u32[]{:S(2)}, u32[]{:S(2)}) collective-permute-start(f32[1,10,130]{2,1,0:T(8,128)S(1)} %get-tuple-element.234), channel_id=1, source_target_pairs={{1,0},{2,1},{3,2},{0,3},{5,4},{6,5},{7,6},{4,7},{9,8},{10,9},{11,1... | collective-permute-start | bytes 15608 | tf_op jit(solution)/shard_map/ppermute | solution.py:18
  38.7 27.7 %collective-permute-start.11 = (f32[1,10,130]{2,1,0:T(8,128)S(1)}, f32[1,10,130]{2,1,0:T(8,128)S(1)}, u32[]{:S(2)}, u32[]{:S(2)}) collective-permute-start(f32[1,10,130]{2,1,0:T(8,128)S(1)} %get-tuple-element.235), channel_id=1, source_target_pairs={{0,1},{1,2},{2,3},{3,0},{4,5},{5,6},{6,7},{7,4},{8,9},{9,10},{10,1... | collective-permute-start | bytes 15608 | tf_op jit(solution)/shard_map/ppermute | solution.py:15
  64.3 14.9 collective-permute-start.9
  64.6 16.4 collective-permute-start.10
  303.1 16.8 collective-permute-start.14
  305.5 23.7 %collective-permute-start.15 = (f32[64,8,1,130]{3,1,2,0:T(8,128)S(1)}, f32[64,8,1,130]{3,1,2,0:T(8,128)S(1)}, u32[]{:S(2)}, u32[]{:S(2)}) collective-permute-start(f32[64,8,1,130]{3,1,2,0:T(8,128)S(1)} %get-tuple-element.215), channel_id=1, source_target_pairs={{4,0},{8,4},{12,8},{0,12},{5,1},{9,5},{13,9},{1,13},{6,2},{10,6},{... | collective-permute-start | bytes 798728 | tf_op jit(solution)/shard_map/ppermute | solution.py:18
  333.5 15.1 collective-permute-start.16
  333.6 16.1 collective-permute-start.17
  575.8 16.7 collective-permute-start.20
  576.4 24.4 %collective-permute-start.21 = (f32[64,8,1,130]{3,1,2,0:T(8,128)S(1)}, f32[64,8,1,130]{3,1,2,0:T(8,128)S(1)}, u32[]{:S(2)}, u32[]{:S(2)}) collective-permute-start(f32[64,8,1,130]{3,1,2,0:T(8,128)S(1)} %get-tuple-element.213), channel_id=1, source_target_pairs={{4,0},{8,4},{12,8},{0,12},{5,1},{9,5},{13,9},{1,13},{6,2},{10,6},{... | collective-permute-start | bytes 798728 | tf_op jit(solution)/shard_map/ppermute | solution.py:18
  605.1 15.1 collective-permute-start.22
  605.2 16.1 collective-permute-start.23
  845.7 16.7 collective-permute-start.26
  847.0 24.6 %collective-permute-start.27 = (f32[64,8,1,130]{3,1,2,0:T(8,128)S(1)}, f32[64,8,1,130]{3,1,2,0:T(8,128)S(1)}, u32[]{:S(2)}, u32[]{:S(2)}) collective-permute-start(f32[64,8,1,130]{3,1,2,0:T(8,128)S(1)} %get-tuple-element.211), channel_id=1, source_target_pairs={{4,0},{8,4},{12,8},{0,12},{5,1},{9,5},{13,9},{1,13},{6,2},{10,6},{... | collective-permute-start | bytes 798728 | tf_op jit(solution)/shard_map/ppermute | solution.py:18
  875.8 15.4 collective-permute-start.28
  876.0 16.4 collective-permute-start.29
  1116.4 16.7 collective-permute-start.32
  1117.9 24.1 %collective-permute-start.33 = (f32[64,8,1,130]{3,1,2,0:T(8,128)S(1)}, f32[64,8,1,130]{3,1,2,0:T(8,128)S(1)}, u32[]{:S(2)}, u32[]{:S(2)}) collective-permute-start(f32[64,8,1,130]{3,1,2,0:T(8,128)S(1)} %get-tuple-element.209), channel_id=1, source_target_pairs={{4,0},{8,4},{12,8},{0,12},{5,1},{9,5},{13,9},{1,13},{6,2},{10,6},{... | collective-permute-start | bytes 798728 | tf_op jit(solution)/shard_map/ppermute | solution.py:18
  1146.3 15.4 collective-permute-start.34
  1146.5 16.4 collective-permute-start.35
  1387.1 16.7 collective-permute-start.38
  1387.7 24.0 %collective-permute-start.39 = (f32[64,8,1,130]{3,1,2,0:T(8,128)S(1)}, f32[64,8,1,130]{3,1,2,0:T(8,128)S(1)}, u32[]{:S(2)}, u32[]{:S(2)}) collective-permute-start(f32[64,8,1,130]{3,1,2,0:T(8,128)S(1)} %get-tuple-element.207), channel_id=1, source_target_pairs={{4,0},{8,4},{12,8},{0,12},{5,1},{9,5},{13,9},{1,13},{6,2},{10,6},{... | collective-permute-start | bytes 798728 | tf_op jit(solution)/shard_map/ppermute | solution.py:18
  1416.0 15.4 collective-permute-start.40
  1416.1 16.4 collective-permute-start.41
  1657.6 16.7 collective-permute-start.44
  1658.8 24.1 %collective-permute-start.45 = (f32[64,8,1,130]{3,1,2,0:T(8,128)S(1)}, f32[64,8,1,130]{3,1,2,0:T(8,128)S(1)}, u32[]{:S(2)}, u32[]{:S(2)}) collective-permute-start(f32[64,8,1,130]{3,1,2,0:T(8,128)S(1)} %get-tuple-element.205), channel_id=1, source_target_pairs={{4,0},{8,4},{12,8},{0,12},{5,1},{9,5},{13,9},{1,13},{6,2},{10,6},{... | collective-permute-start | bytes 798728 | tf_op jit(solution)/shard_map/ppermute | solution.py:18
  1687.2 15.2 collective-permute-start.46
  1687.3 16.2 collective-permute-start.47
  (39 other events, 780.7 us)
